TPU v7x, 512 devices: a whole 4x8x8 slice. The times are simulated.
512 devices in a mesh: dp: 16 (over x, y_lo), seq: 32 (over z, y_hi, core).
Axes of the slice: x: 4, y: 8 (y_hi: 2, y_lo: 4; y = y_hi * 4 + y_lo), z: 8, core: 2. Of those that a mesh axis runs over, the one named last changes fastest.
Arguments:
- inputs: bfloat16 [16, 16384, 1024], P('dp', 'seq'), may hold values from -6 to 6
- cotangent: bfloat16 [16, 16384, 1024], P('dp', 'seq'), may hold values from -6 to 6
- block_right: bfloat16 [32, 512, 512], P('seq'), may hold values from -0.25 to 0.25
- block_left: bfloat16 [512, 32, 32], P('seq'), may hold values from -1 to 1
- gate_in: float32 [1024], replicated, may hold values from 0.1 to 1.9
- gate_out: float32 [1024], replicated, may hold values from -3 to 3
Outputs:
- d_inputs: bfloat16 [16, 16384, 1024], P('dp', 'seq')
- d_right: float32 [32, 512, 512], P('seq')
- d_left: float32 [512, 32, 32], P('seq')
- d_gate_in: float32 [1024], replicated
- d_gate_out: float32 [1024], replicated
All inputs are finite; a program needn't handle non-finite values.
Results may differ from a plain program's by a relative error of at most 0.006.
Values may be sent and summed in bfloat16 or wider, within the bound.
A program may use at most 64 MiB of HBM per device.

v0:
```python
import jax
import jax.numpy as jnp
from jax import lax
from jax.sharding import PartitionSpec as P


def on_device(inputs, cotangent, block_right, block_left, gate_in, gate_out):
    samples, positions, channels = inputs.shape
    order = block_right.shape[1]
    local_blocks = positions // order
    shape_four = (samples, local_blocks, order, channels)
    input_rows = inputs.reshape(shape_four)
    cot_rows = cotangent.reshape(shape_four)
    input_wide = input_rows.astype(jnp.float32)
    hidden = (input_wide * gate_in).astype(jnp.bfloat16)
    mixed = jnp.einsum(
        "kcb,nkbd->nkcd", block_right, hidden, preferred_element_type=jnp.float32
    ).astype(jnp.bfloat16)
    pieces = lax.all_to_all(mixed, "seq", split_axis=2, concat_axis=1, tiled=True)
    mixed_cols = pieces
    monarch_cols = jnp.einsum(
        "cea,nacd->necd", block_left, pieces, preferred_element_type=jnp.float32
    ).astype(jnp.bfloat16)
    monarch = lax.all_to_all(monarch_cols, "seq", split_axis=1, concat_axis=2, tiled=True)
    sig = jax.nn.sigmoid(input_wide * gate_out)
    cot_wide = cot_rows.astype(jnp.float32)
    d_monarch = (cot_wide * sig).astype(jnp.bfloat16)
    d_pre = cot_wide * monarch.astype(jnp.float32) * sig * (1.0 - sig)
    gate_grad = lax.optimization_barrier((d_pre * gate_out).astype(jnp.bfloat16)).astype(
        jnp.float32
    )
    gout_part = jnp.sum(d_pre * input_wide, axis=(0, 1, 2))
    dmon_cols = lax.all_to_all(d_monarch, "seq", split_axis=2, concat_axis=1, tiled=True)
    dmix_cols = jnp.einsum(
        "cea,necd->nacd", block_left, dmon_cols, preferred_element_type=jnp.float32
    ).astype(jnp.bfloat16)
    left_part = jnp.einsum(
        "necd,nacd->cea", dmon_cols, mixed_cols, preferred_element_type=jnp.float32
    )
    pieces = lax.all_to_all(dmix_cols, "seq", split_axis=1, concat_axis=2, tiled=True)
    d_hidden = jnp.einsum("kcb,nkcd->nkbd", block_right, pieces, preferred_element_type=jnp.float32)
    d_inputs = (gate_grad + d_hidden * gate_in).astype(jnp.bfloat16).reshape(inputs.shape)
    gin_part = jnp.sum(d_hidden * input_wide, axis=(0, 1, 2))
    right_part = jnp.einsum("nkcd,nkbd->kcb", pieces, hidden, preferred_element_type=jnp.float32)
    right_sum, left_sum = lax.psum((right_part, left_part), "dp")
    gin_sum, gout_sum = lax.psum((gin_part, gout_part), ("dp", "seq"))
    batch_total = samples * lax.axis_size("dp")
    token_total = positions * lax.axis_size("seq")
    factor_scale = 1.0 / jnp.sqrt(jnp.float32(batch_total * channels))
    gate_scale = 1.0 / jnp.sqrt(jnp.float32(batch_total * token_total))
    return (
        d_inputs,
        right_sum * factor_scale,
        left_sum * factor_scale,
        gin_sum * gate_scale,
        gout_sum * gate_scale,
    )


def solution(mesh):
    in_specs = (
        P("dp", "seq", None),
        P("dp", "seq", None),
        P("seq", None, None),
        P("seq", None, None),
        P(),
        P(),
    )
    out_specs = (P("dp", "seq", None), P("seq", None, None), P("seq", None, None), P(), P())
    return jax.shard_map(
        on_device, mesh=mesh, in_specs=in_specs, out_specs=out_specs, check_vma=False
    )
```

profile of v0, /device:TPU:64, one launch (start us, length us, event | category | flops | bytes accessed | tf_op | source)
XLA Modules:
  0.0 406.4 jit_solution(17450820852636127859)
XLA Ops:
  7.2 0.0 copy-start
  7.2 1.0 copy-done
  8.2 3.0 fusion.26
  11.2 4.7 %copy.24 = bf16[1,1,512,1024]{3,0,1,2:T(2,128)(2,1)S(1)} copy(bf16[1,1,512,1024]{2,3,0,1:T(8,128)(2,1)} %fusion.26) | data formatting | bytes 2097152 | tf_op jit(solution)/shard_map/convert_element_type | solution.py:18
  15.9 0.5 broadcast.153
  16.4 7.8 %reduce.1 = bf16[512,1024]{1,0:T(8,128)(2,1)} reduce(bf16[512,1,1,1024]{3,2,1,0:T(2,128)(2,1)S(1)} %bitcast.97, bf16[]{:T(256)} %broadcast.153), dimensions={1,2}, to_apply=%bitcast.85.reduce_sub_computation | reduce | bytes 2097154
  24.2 1.8 reshape.301
  26.0 44.4 %all_to_all.16 = bf16[32,2,8192]{2,1,0:T(2,128)(2,1)} all-to-all(bf16[32,2,8192]{2,1,0:T(2,128)(2,1)S(1)} %reshape.301), channel_id=1, replica_groups=mesh['dp'=16,'seq'=32] {'seq'}, dimensions={0} | all-to-all | bytes 2097152 | tf_op jit(solution)/shard_map/all_to_all | solution.py:19
  70.4 4.3 %reshape.302 = bf16[512,1,1,1024]{3,2,1,0:T(2,128)(2,1)S(1)} reshape(bf16[32,2,8192]{2,1,0:T(2,128)(2,1)} %all_to_all.16) | data formatting | bytes 2097152
  74.7 0.0 copy-start.6
  74.7 0.4 copy.36
  75.1 0.0 copy-start.1
  75.1 0.5 copy-done.6
  75.6 1.5 fusion.25
  77.2 0.6 copy.26
  77.8 0.0 copy-done.1
  77.8 0.0 copy-start.2
  77.8 0.0 copy-start.3
  77.8 0.0 copy-start.8
  77.8 35.6 %all_to_all.17 = bf16[1,32,16,1024]{3,2,0,1:T(8,128)(2,1)S(1)} all-to-all(bf16[1,32,16,1024]{3,2,0,1:T(8,128)(2,1)S(1)} %copy.26), channel_id=1, replica_groups=mesh['dp'=16,'seq'=32] {'seq'}, dimensions={1} | all-to-all | bytes 2097152 | tf_op jit(solution)/shard_map/all_to_all | solution.py:24
  113.4 0.2 bitcast_convert_fusion
  113.6 0.0 copy-done.2
  113.7 0.0 copy-done.3
  113.7 0.0 copy-done.8
  113.7 2.0 fusion.12
  115.7 2.9 copy.47
  118.7 9.0 %reduce.2 = bf16[512,1024]{1,0:T(8,128)(2,1)} reduce(bf16[512,1,1,1024]{3,2,1,0:T(2,128)(2,1)} %bitcast.98, bf16[]{:T(256)} %broadcast.153), dimensions={1,2}, to_apply=%bitcast.94.reduce_sub_computation | reduce | bytes 2097154
  127.7 2.6 reshape.299
  130.3 36.7 %all_to_all.18 = bf16[32,2,8192]{2,1,0:T(2,128)(2,1)} all-to-all(bf16[32,2,8192]{2,1,0:T(2,128)(2,1)} %reshape.299), channel_id=1, replica_groups=mesh['dp'=16,'seq'=32] {'seq'}, dimensions={0} | all-to-all | bytes 2097152 | tf_op jit(solution)/shard_map/all_to_all | solution.py:33
  167.0 5.8 %reshape.300 = bf16[512,1,1,1024]{3,2,1,0:T(2,128)(2,1)} reshape(bf16[32,2,8192]{2,1,0:T(2,128)(2,1)} %all_to_all.18) | data formatting | bytes 2097152
  172.8 2.9 copy.37
  175.7 2.7 fusion.24
  178.4 1.6 copy.32
  180.0 0.0 copy-start.9
  180.0 10.2 %all-to-all-start.3 = ((bf16[1,32,16,1024]{3,2,0,1:T(8,128)(2,1)}), bf16[1,32,16,1024]{3,2,0,1:T(8,128)(2,1)}, u32[]{:S(2)}, u32[]{:S(2)}) async-start(bf16[1,32,16,1024]{3,2,0,1:T(8,128)(2,1)} %copy.32), calls=%async_computation.3 | async-start | bytes 2097152 | tf_op jit(solution)/shard_map/all_to_all | solution.py:40
  190.2 0.0 all-reduce.4.cloned.1.call-start
  190.2 3.5 fusion.29
  193.7 24.2 %all-to-all-done.3 = bf16[1,32,16,1024]{3,2,0,1:T(8,128)(2,1)} async-done(((bf16[1,32,16,1024]{3,2,0,1:T(8,128)(2,1)}), bf16[1,32,16,1024]{3,2,0,1:T(8,128)(2,1)}, u32[]{:S(2)}, u32[]{:S(2)}) %all-to-all-start.3) | async-done | bytes 1048608 | tf_op jit(solution)/shard_map/all_to_all | solution.py:40
  217.9 0.0 copy-done.9
  217.9 3.3 convolution_bitcast_fusion
  221.2 0.0 all-reduce.4.cloned.1.call-update
  221.2 0.0 copy-start.4
  221.2 0.0 copy-start.5
  221.2 2.6 fusion.21
  223.8 0.0 copy-done.4
  223.8 0.0 copy-done.5
  223.8 3.1 fusion.8
  227.0 101.5 %all-reduce = (f32[1024]{0:T(1024)S(1)}, f32[1024]{0:T(1024)S(1)}) all-reduce(f32[1024]{0:T(1024)S(1)} %get-tuple-element.11, f32[1024]{0:T(1024)S(1)} %fusion.21), channel_id=1, replica_groups=mesh['dp'=16,'seq'=32] {'dp','seq'}, use_global_device_ids=true, to_apply=%region_3.0 | all-reduce | flops 2048 | bytes 16384 | tf_op jit(solution)/shard_map/psum | solution.py:46
  328.5 0.6 broadcast_multiply_fusion.2
  329.1 67.4 %all-reduce.4.cloned.1.call-done = (f32[1,512,512]{2,1,0:T(8,128)}, f32[16,32,32]{2,1,0:T(8,128)}) async-done(((f32[1,512,512]{2,1,0:T(8,128)}, f32[16,32,32]{2,1,0:T(8,128)}), (f32[1,512,512]{2,1,0:T(8,128)}, f32[16,32,32]{2,1,0:T(8,128)})) %all-reduce.4.cloned.1.call-update) | async-done | bytes 1114128 | tf_op jit(solution)/shard_map/psum | solution.py:45
  396.5 0.0 copy-start.7
  396.5 2.3 broadcast_multiply_fusion
  398.9 0.0 copy-done.7
  398.9 0.7 broadcast_multiply_fusion.1
Async XLA Ops:
  7.2 1.0 copy-start
  74.7 0.9 copy-start.6
  75.1 2.6 copy-start.1
  77.8 35.9 %copy-start.2 = (bf16[1,512,1024]{2,1,0:T(8,128)(2,1)S(1)}, bf16[1,512,1024]{2,1,0:T(8,128)(2,1)}, u32[]{:S(2)}) copy-start(bf16[1,512,1024]{2,1,0:T(8,128)(2,1)} %param.7) | copy-start | bytes 3145732
  77.8 35.9 %copy-start.3 = (bf16[1,512,1024]{2,1,0:T(8,128)(2,1)S(1)}, bf16[1,512,1024]{2,1,0:T(8,128)(2,1)}, u32[]{:S(2)}) copy-start(bf16[1,512,1024]{2,1,0:T(8,128)(2,1)} %param.6) | copy-start | bytes 3145732
  77.8 35.9 %copy-start.8 = (f32[1024]{0:T(1024)S(1)}, f32[1024]{0:T(1024)}, u32[]{:S(2)}) copy-start(f32[1024]{0:T(1024)} %param.11) | copy-start | bytes 12292
  180.0 37.9 %copy-start.9 = (f32[1024]{0:T(1024)S(1)}, f32[1024]{0:T(1024)}, u32[]{:S(2)}) copy-start(f32[1024]{0:T(1024)} %param.10) | copy-start | bytes 12292
  180.0 37.9 %all-to-all-start.3 = ((bf16[1,32,16,1024]{3,2,0,1:T(8,128)(2,1)}), bf16[1,32,16,1024]{3,2,0,1:T(8,128)(2,1)}, u32[]{:S(2)}, u32[]{:S(2)}) async-start(bf16[1,32,16,1024]{3,2,0,1:T(8,128)(2,1)} %copy.32), calls=%async_computation.3 | async-start | bytes 2097152 | tf_op jit(solution)/shard_map/all_to_all | solution.py:40
  190.2 206.3 %all-reduce.4.cloned.1.call-start = ((), (), s32[]{:S(2)}) async-start(), calls=%async_computation.4 | async-start | bytes 2621440 | tf_op jit(solution)/shard_map/psum | solution.py:45
  221.2 2.6 copy-start.4
  221.2 2.6 copy-start.5
  396.5 2.3 copy-start.7
Sparse Core Ops, SparseCore 0:
  221.3 175.1 all-reduce.3
where the time goes:
time: 408 us; the launch traced here: 406 us
  blocking collectives  218 us (53%)
  waiting for transfers between devices  91.6 us (22%)
  local copies, waits for them, and re-layouts  29.8 us (7%)
  other arithmetic  25.3 us (6%)
  matrix products  17.1 us (4%)
  between operations  14.2 us (3%)
  starting transfers between devices  10.2 us (2%)
    psum x1, blocking collectives, on_device(): gin_sum, gout_sum = lax.psum((gin_part, gout_part), ('dp', 'seq'))  102 us
    psum x1, waiting for transfers between devices, on_device(): right_sum, left_sum = lax.psum((right_part, left_part), 'dp')  67.4 us
    all_to_all x1, blocking collectives, on_device(): lax.all_to_all(mixed, 'seq', split_axis=2, concat_axis=1, tiled=True)  44.4 us
    all_to_all x1, blocking collectives, on_device(): lax.all_to_all(d_monarch, 'seq', split_axis=2, concat_axis=1, tiled=True)  36.7 us
    all_to_all x1, blocking collectives, on_device(): lax.all_to_all(monarch_cols, 'seq', split_axis=1, concat_axis=2, tiled=True)  35.6 us
    all_to_all x1, waiting for transfers between devices, on_device(): lax.all_to_all(dmix_cols, 'seq', split_axis=1, concat_axis=2, tiled=True)  24.2 us
    unnamed x27, local copies, waits for them, and re-layouts  19.9 us
    unnamed x2, other arithmetic  16.8 us
  transfers between devices with their start and end apart: 2, of which 2 were waited for; matrix products, arithmetic and copies ran while one was open for 2% of the time, Pallas kernels for 0%

commit v1 on v0

v1 whole, which is shorter than its diff:
```python
import functools

import jax
import jax.numpy as jnp
from jax import lax
from jax.experimental import pallas as pl
from jax.experimental.pallas import tpu as pltpu
from jax.sharding import PartitionSpec as P

MESH = pl.DeviceIdType.MESH
F32 = jnp.float32
BF16 = jnp.bfloat16
K = 4
D = 1024
CH = D // K
N = 512
DMON, MIX, DMIX, MON = 0, 1, 2, 3
NT = (((1,), (1,)), ((), ()))


def dot(a, b):
    return jnp.dot(a, b, preferred_element_type=F32)


def dot_nt(a, b):
    return lax.dot_general(a, b, NT, preferred_element_type=F32)


def natural(p):
    return ((p // 2) % 8) * 4 + (p // 16) * 2 + p % 2


def iota(shape, dim):
    return lax.broadcasted_iota(jnp.int32, shape, dim)


def kernel(
    x_hbm, c_hbm, r_hbm, l_ref, gi_ref, go_ref,
    o_hbm, dr_hbm, dl_ref, dgi_ref, dgo_ref,
    xv, cv, hv, p1, dh, out, rr, rt, ww, wt,
    tbuf, sbuf, rbuf, racc, lacc, gacc,
    gxs, gxr, gys, gyr, fin, drv, lx, ly, ga, gb, gc,
    in_sem, out_sem, ys, yr, zs, zr, rs_s, rs_r, sm_s, sm_r,
):
    dp = lax.axis_index("dp")
    seq = lax.axis_index("seq")
    xx, yl = dp // 4, dp % 4
    z, yh, core = seq // 4, (seq // 2) % 2, seq % 2
    oth = 1 - yh
    me = z * 2 + core
    ring = yh * 4 + yl

    def zc_peer(q):
        return (dp, (q // 2) * 4 + yh * 2 + q % 2)

    def x_peer(q):
        return (q * 4 + yl, seq)

    def y_peer(q):
        return (xx * 4 + q % 4, z * 4 + (q // 4) * 2 + core)

    partner = (dp, z * 4 + oth * 2 + core)

    def load_x(k):
        return pltpu.make_async_copy(x_hbm.at[0, :, pl.ds(k * CH, CH)], xv.at[k], in_sem.at[k])

    def load_c(k):
        return pltpu.make_async_copy(c_hbm.at[0, :, pl.ds(k * CH, CH)], cv.at[k], in_sem.at[K + k])

    def load_r(h):
        return pltpu.make_async_copy(r_hbm.at[:, h], rr.at[h], in_sem.at[2 * K + h])

    for k in range(K):
        load_x(k).start()
        load_c(k).start()
    for h in range(2):
        load_r(h).start()

    barrier = pltpu.get_barrier_semaphore()

    def greet(peer_of, mine, n):
        def step(i, _):
            pl.semaphore_signal(
                barrier, inc=1, device_id=peer_of(lax.rem(mine + i, n)), device_id_type=MESH
            )
            return 0

        lax.fori_loop(1, n, step, 0)

    greet(zc_peer, me, 16)
    greet(x_peer, xx, 4)
    greet(y_peer, ring, 8)

    def y_copy(s):
        return pltpu.make_async_remote_copy(
            src_ref=tbuf.at[s],
            dst_ref=sbuf.at[s, yh],
            send_sem=ys.at[s],
            recv_sem=yr.at[s],
            device_id=partner,
            device_id_type=MESH,
        )

    def y_arrived(s):
        pltpu.make_async_copy(sbuf.at[s, oth], sbuf.at[s, oth], yr.at[s]).wait()

    def z_send(s):
        pltpu.make_async_copy(sbuf.at[s, :, me], rbuf.at[s, :, me], zr.at[s]).start()

        def step(i, _):
            q = lax.rem(me + i, 16)
            pltpu.make_async_remote_copy(
                src_ref=sbuf.at[s, :, q],
                dst_ref=rbuf.at[s, :, me],
                send_sem=zs.at[s],
                recv_sem=zr.at[s],
                device_id=zc_peer(q),
                device_id_type=MESH,
            ).start()
            return 0

        lax.fori_loop(1, 16, step, 0)

    def z_arrived(s):
        pltpu.make_async_copy(rbuf.at[s], rbuf.at[s], zr.at[s]).wait()

    def sends_done(s, _):
        y_copy(s).wait_send()
        pltpu.make_async_copy(sbuf.at[s, :, pl.ds(0, 15)], sbuf.at[s, :, pl.ds(0, 15)], zs.at[s]).wait()
        return 0

    def gates(k):
        lanes = pl.ds(pl.multiple_of(k * CH, CH), CH)
        return gi_ref[:, lanes], go_ref[:, lanes]

    def make_dmon(k, h, mine):
        _, go = gates(k)

        def step(j, _):
            row = pl.ds(pl.multiple_of(j * 64 + h * 32, 32), 32)
            xw = xv[k, row, :].astype(F32)
            cw = cv[k, row, :].astype(F32)
            sig = jax.nn.sigmoid(xw * go)
            dm = cw * sig
            p1[k, row, :] = dm * (1.0 - sig)
            piece = dm.astype(BF16).reshape(2, 16, CH)
            if mine:
                sbuf[DMON * K + k, h, pl.ds(j * 2, 2)] = piece
            else:
                tbuf[DMON * K + k, pl.ds(j * 2, 2)] = piece
            return 0

        lax.fori_loop(0, 8, step, 0)

    def make_halves(s, left, right):
        tbuf[s] = dot(left[oth], right).astype(BF16).reshape(16, 16, CH)
        sbuf[s, yh] = dot(left[yh], right).astype(BF16).reshape(16, 16, CH)

    def make_hidden(k):
        gi, _ = gates(k)

        def step(j, _):
            row = pl.ds(pl.multiple_of(j * 32, 32), 32)
            hv[k, row, :] = (xv[k, row, :].astype(F32) * gi).astype(BF16)
            return 0

        lax.fori_loop(0, 16, step, 0)

    def make_mix(k):
        make_hidden(k)
        make_halves(MIX * K + k, rr2, hv[k])

    rr2 = rr.reshape(2, 256, N)

    def flat(s):
        return rbuf[s].reshape(N, CH)

    def on_dmon(k):
        make_halves(DMIX * K + k, wt, flat(DMON * K + k))

    def on_mix(k):
        m = flat(MIX * K + k)
        make_halves(MON * K + k, ww, m)
        lacc[...] += dot_nt(m, flat(DMON * K + k))

    def fold(v):
        return v.reshape(4, 8, CH).sum(axis=0)

    def on_dmix(k):
        dm = flat(DMIX * K + k)
        dh[k] = dot(rt[...], dm)
        racc[...] += dot_nt(dm, hv[k])

        def step(j, acc):
            row = pl.ds(pl.multiple_of(j * 32, 32), 32)
            return acc + fold(dh[k, row, :] * xv[k, row, :].astype(F32))

        acc = lax.fori_loop(0, 16, step, jnp.zeros((8, CH), F32))
        gacc[k, 0:1, :] = acc.sum(axis=0, keepdims=True)

    def store_out(k):
        return pltpu.make_async_copy(out.at[k], o_hbm.at[0, :, pl.ds(k * CH, CH)], out_sem.at[k])

    def on_mon(k):
        gi, go = gates(k)

        def step(j, acc):
            h, w = j // 8, j % 8
            row = pl.ds(pl.multiple_of(w * 64 + h * 32, 32), 32)
            mon = rbuf[MON * K + k, h, pl.ds(w * 2, 2)].reshape(32, CH).astype(F32)
            dpre = p1[k, row, :] * mon
            gg = (dpre * go).astype(BF16).astype(F32)
            out[k, row, :] = (gg + dh[k, row, :] * gi).astype(BF16)
            return acc + fold(dpre * xv[k, row, :].astype(F32))

        acc = lax.fori_loop(0, 16, step, jnp.zeros((8, CH), F32))
        gacc[k, 1:2, :] = acc.sum(axis=0, keepdims=True)

    def spread(buf, i_sem, peer_of, mine, n):
        def step(i, _):
            pltpu.make_async_remote_copy(
                src_ref=buf.at[mine],
                dst_ref=buf.at[mine],
                send_sem=sm_s.at[i_sem],
                recv_sem=sm_r.at[i_sem],
                device_id=peer_of(lax.rem(mine + i, n)),
                device_id_type=MESH,
            ).start()
            return 0

        lax.fori_loop(1, n, step, 0)

    def spread_wait(buf, i_sem, n):
        part = buf.at[pl.ds(0, n - 1)]
        pltpu.make_async_copy(part, part, sm_r.at[i_sem]).wait()
        pltpu.make_async_copy(part, part, sm_s.at[i_sem]).wait()

    def scatter(src, dst, i_sem, peer_of, mine):
        def step(i, _):
            q = lax.rem(mine + i, 4)
            pltpu.make_async_remote_copy(
                src_ref=src.at[q],
                dst_ref=dst.at[mine],
                send_sem=rs_s.at[i_sem],
                recv_sem=rs_r.at[i_sem],
                device_id=peer_of(q),
                device_id_type=MESH,
            ).start()
            return 0

        lax.fori_loop(1, 4, step, 0)

    def scatter_wait(src, dst, i_sem):
        got, sent = dst.at[pl.ds(0, 3)], src.at[pl.ds(0, 3)]
        pltpu.make_async_copy(got, got, rs_r.at[i_sem]).wait()
        pltpu.make_async_copy(sent, sent, rs_s.at[i_sem]).wait()

    def yl_peer(q):
        return (xx * 4 + q, seq)

    def build_left():
        r, c = iota((N, N), 0), iota((N, N), 1)
        perm = ((r % 16 == c // 32) & (natural(r // 16) == c % 32)).astype(F32).astype(BF16)
        rows = dot(perm, l_ref[...].reshape(N, 32)).astype(BF16)
        e = iota((32, N), 0) == natural(iota((32, N), 1) // 16)
        wide = dot(rows, e.astype(F32).astype(BF16))
        w = jnp.where(r % 16 == c % 16, wide, 0.0).astype(BF16)
        eye = (r == c).astype(F32).astype(BF16)
        ww[...] = w.reshape(2, 256, N)
        wt[...] = dot_nt(eye, w).astype(BF16).reshape(2, 256, N)
        rt[...] = dot_nt(eye, rr[...].reshape(N, N)).astype(BF16)

    def split(v):
        hi = v.astype(BF16)
        rest = v - hi.astype(F32)
        mid = rest.astype(BF16)
        return hi, mid, (rest - mid.astype(F32)).astype(BF16)

    def left_grad():
        r, c = iota((N, N), 0), iota((N, N), 1)
        kept = jnp.where(r % 16 == c % 16, lacc[...], 0.0)
        e = (iota((32, N), 0) == iota((32, N), 1) // 16).astype(F32).astype(BF16)
        hi, mid, low = split(kept)
        lx[xx] = dot(e, hi) + dot(e, mid) + dot(e, low)

    def left_out():
        g = (ly[0] + ly[1] + ly[2] + ly[3]) * (1.0 / 128.0)
        r, c = iota((N, N), 0), iota((N, N), 1)
        perm = ((c % 16 == r // 32) & (natural(c // 16) == r % 32)).astype(F32).astype(BF16)
        cols = (natural(iota((32, 32), 0)) == iota((32, 32), 1)).astype(F32).astype(BF16)
        total = jnp.zeros((N, 32), F32)
        for part in split(g):
            total = total + dot(dot_nt(perm, part).astype(BF16), cols)
        dl_ref[...] = total.reshape(16, 32, 32)

    def right_1():
        gxs[...] = racc[...].astype(BF16).reshape(4, 128, N)
        scatter(gxs, gxr, 0, x_peer, xx)

    def right_2():
        scatter_wait(gxs, gxr, 0)
        own = racc[pl.ds(pl.multiple_of(xx * 128, 128), 128), :]
        for i in range(1, 4):
            own = own + gxr[lax.rem(xx + i, 4)].astype(F32)
        racc[0:128, :] = own
        gys[...] = own.astype(BF16).reshape(4, 32, N)
        scatter(gys, gyr, 1, yl_peer, yl)

    def right_3():
        scatter_wait(gys, gyr, 1)
        own = racc[pl.ds(pl.multiple_of(yl * 32, 32), 32), :]
        for i in range(1, 4):
            own = own + gyr[lax.rem(yl + i, 4)].astype(F32)
        fin[xx, yl] = (own * (1.0 / 128.0)).astype(BF16)
        spread(fin.at[xx], 2, yl_peer, yl, 4)

    def right_4():
        spread_wait(fin.at[xx], 2, 4)
        spread(fin, 3, x_peer, xx, 4)

    right_store = pltpu.make_async_copy(drv, dr_hbm, out_sem.at[K])

    def right_5():
        spread_wait(fin, 3, 4)

        def step(j, _):
            drv[j % 8, j // 8] = fin[j // 4, j % 4].astype(F32)
            return 0

        lax.fori_loop(0, 16, step, 0)
        right_store.start()

    lacc[...] = jnp.zeros_like(lacc)
    racc[...] = jnp.zeros_like(racc)
    for k in range(K):
        load_x(k).wait()
        load_c(k).wait()
        make_dmon(k, oth, False)
        if k == 0:
            pl.semaphore_wait(barrier, 25)
        if k < 2:
            y_copy(k).start()
        make_dmon(k, yh, True)
    for h in range(2):
        load_r(h).wait()
    make_mix(0)
    build_left()

    last = 4 * K

    def slot(t):
        y_arrived(t)

        @pl.when(t + 2 < last)
        def _():
            y_copy(t + 2).start()

        z_send(t)

    slot(0)

    def phase_dmon(k, _):
        make_mix(k)
        slot(DMON * K + k)
        z_arrived(DMON * K + k - 1)
        on_dmon(k - 1)
        return 0

    lax.fori_loop(1, K, phase_dmon, 0)
    slot(MIX * K)
    z_arrived(MIX * K - 1)
    on_dmon(K - 1)

    def phase_mix(k, _):
        slot(MIX * K + k)
        z_arrived(MIX * K + k - 1)
        on_mix(k - 1)
        return 0

    lax.fori_loop(1, K, phase_mix, 0)
    slot(DMIX * K)
    z_arrived(DMIX * K - 1)
    on_mix(K - 1)
    left_grad()
    spread(lx, 0, x_peer, xx, 4)

    def phase_dmix(k, _):
        slot(DMIX * K + k)
        z_arrived(DMIX * K + k - 1)
        on_dmix(k - 1)
        return 0

    lax.fori_loop(1, K, phase_dmix, 0)
    spread_wait(lx, 0, 4)
    ly[yl] = lx[0] + lx[1] + lx[2] + lx[3]
    spread(ly, 1, yl_peer, yl, 4)

    slot(MON * K)
    z_arrived(MON * K - 1)
    on_dmix(K - 1)
    right_1()
    for k in range(1, K):
        slot(MON * K + k)
        z_arrived(MON * K + k - 1)
        on_mon(k - 1)
        store_out(k - 1).start()
        if k == 1:
            right_2()
            spread_wait(ly, 1, 4)
            left_out()
        if k == 2:
            right_3()
        if k == 3:
            right_4()
    z_arrived(last - 1)
    on_mon(K - 1)
    store_out(K - 1).start()
    ga[me] = jnp.concatenate([gacc[k] for k in range(K)], axis=1)
    spread(ga, 4, zc_peer, me, 16)
    right_5()
    spread_wait(ga, 4, 16)
    gb[xx] = ga[...].sum(axis=0)
    spread(gb, 5, x_peer, xx, 4)
    spread_wait(gb, 5, 4)
    gc[ring] = gb[...].sum(axis=0)
    spread(gc, 6, y_peer, ring, 8)
    spread_wait(gc, 6, 8)
    total = gc[...].sum(axis=0) * (1.0 / 512.0)
    dgi_ref[...] = total[0:1]
    dgo_ref[...] = total[1:2]
    lax.fori_loop(0, last, sends_done, 0)
    for k in range(K):
        store_out(k).wait()
    right_store.wait()


def on_device(inputs, cotangent, block_right, block_left, gate_in, gate_out):
    hbm = pl.BlockSpec(memory_space=pl.ANY)
    vmem = pl.BlockSpec(memory_space=pltpu.VMEM)
    sub = 4 * K
    scratch = [
        pltpu.VMEM((K, N, CH), BF16),
        pltpu.VMEM((K, N, CH), BF16),
        pltpu.VMEM((K, N, CH), BF16),
        pltpu.VMEM((K, N, CH), F32),
        pltpu.VMEM((K, N, CH), F32),
        pltpu.VMEM((K, N, CH), BF16),
        pltpu.VMEM((2, 8, 32, N), BF16),
        pltpu.VMEM((N, N), BF16),
        pltpu.VMEM((2, 256, N), BF16),
        pltpu.VMEM((2, 256, N), BF16),
        pltpu.VMEM((sub, 16, 16, CH), BF16),
        pltpu.VMEM((sub, 2, 16, 16, CH), BF16),
        pltpu.VMEM((sub, 2, 16, 16, CH), BF16),
        pltpu.VMEM((N, N), F32),
        pltpu.VMEM((N, N), F32),
        pltpu.VMEM((K, 2, CH), F32),
        pltpu.VMEM((4, 128, N), BF16),
        pltpu.VMEM((4, 128, N), BF16),
        pltpu.VMEM((4, 32, N), BF16),
        pltpu.VMEM((4, 32, N), BF16),
        pltpu.VMEM((4, 4, 32, N), BF16),
        pltpu.VMEM((8, 2, 32, N), F32),
        pltpu.VMEM((4, 32, N), F32),
        pltpu.VMEM((4, 32, N), F32),
        pltpu.VMEM((16, 2, D), F32),
        pltpu.VMEM((4, 2, D), F32),
        pltpu.VMEM((8, 2, D), F32),
        pltpu.SemaphoreType.DMA((2 * K + 2,)),
        pltpu.SemaphoreType.DMA((K + 1,)),
        pltpu.SemaphoreType.DMA((sub,)),
        pltpu.SemaphoreType.DMA((sub,)),
        pltpu.SemaphoreType.DMA((sub,)),
        pltpu.SemaphoreType.DMA((sub,)),
        pltpu.SemaphoreType.DMA((2,)),
        pltpu.SemaphoreType.DMA((2,)),
        pltpu.SemaphoreType.DMA((7,)),
        pltpu.SemaphoreType.DMA((7,)),
    ]
    d_inputs, d_right, d_left, d_gin, d_gout = pl.pallas_call(
        kernel,
        out_shape=(
            jax.ShapeDtypeStruct((1, N, D), BF16),
            jax.ShapeDtypeStruct((8, 2, 32, N), F32),
            jax.ShapeDtypeStruct((16, 32, 32), F32),
            jax.ShapeDtypeStruct((1, D), F32),
            jax.ShapeDtypeStruct((1, D), F32),
        ),
        in_specs=[hbm, hbm, hbm, vmem, vmem, vmem],
        out_specs=(hbm, hbm, vmem, vmem, vmem),
        scratch_shapes=scratch,
        compiler_params=pltpu.CompilerParams(
            collective_id=0, has_side_effects=True, vmem_limit_bytes=50 * 1024 * 1024
        ),
        name="monarch",
    )(
        inputs,
        cotangent,
        block_right.reshape(8, 2, 32, N),
        block_left,
        gate_in.reshape(1, D),
        gate_out.reshape(1, D),
    )
    return (
        d_inputs,
        d_right.reshape(1, N, N),
        d_left,
        d_gin.reshape(D),
        d_gout.reshape(D),
    )


def solution(mesh):
    in_specs = (
        P("dp", "seq", None),
        P("dp", "seq", None),
        P("seq", None, None),
        P("seq", None, None),
        P(),
        P(),
    )
    out_specs = (P("dp", "seq", None), P("seq", None, None), P("seq", None, None), P(), P())
    return jax.shard_map(
        on_device, mesh=mesh, in_specs=in_specs, out_specs=out_specs, check_vma=False
    )
```

time: 408 us -> 159 us (0.39)
  the two profiles are of different devices: /device:TPU:64 before, /device:TPU:1 now
where the time goes in v1:
time: 159 us; the launch traced here: 158 us
  Pallas kernels  149 us (94%)
  local copies, waits for them, and re-layouts  8.37 us (5%)
    pallas_call x1, Pallas kernels, on_device(): pl.pallas_call(kernel, out_shape=(jax.ShapeDtypeStruct((1, N, D), BF16),...  149 us
    unnamed x15, local copies, waits for them, and re-layouts  8.37 us

profile of v1, /device:TPU:1, one launch (start us, length us, event | category | flops | bytes accessed | tf_op | source)
XLA Modules:
  0.0 158.2 jit_solution(12115308173362926136)
XLA Ops:
  0.6 0.0 copy-start.3
  0.6 0.7 copy-done.3
  1.3 0.0 copy-start
  1.3 1.2 copy-done
  2.5 0.0 copy-start.1
  2.5 1.0 copy-done.1
  3.6 0.0 copy-start.2
  3.6 0.9 copy-done.2
  4.5 0.0 copy-start.4
  4.5 0.7 copy-done.4
  5.2 149.2 %monarch.1 = (bf16[1,512,1024]{2,1,0:T(8,128)(2,1)S(1)}, f32[8,2,32,512]{3,2,1,0:T(8,128)S(1)}, f32[16,32,32]{2,1,0:T(8,128)S(1)}, f32[1,1024]{1,0:T(1,128)S(1)}, f32[1,1024]{1,0:T(1,128)S(1)}) custom-call(bf16[1,512,1024]{2,1,0:T(8,128)(2,1)S(1)} %copy-done, bf16[1,512,1024]{2,1,0:T(8,128)(2,1)} %c_hbm.1, bf16[8,2,32,512]{3,2,1,0:T(8,128)(2,1)S(1)} %bitcast.7, ...), custom_call_target="tpu_custom_call" | custom-call | tf_op jit(solution)/shard_map/monarch/pallas_call | solution.py:480
  154.4 1.0 copy.16
  155.3 1.0 copy.17
  156.3 0.7 copy.18
  157.0 0.6 copy.19
  157.6 0.6 copy.20
Async XLA Ops:
  0.6 0.7 copy-start.3
  1.3 1.2 copy-start
  2.5 1.0 copy-start.1
  3.6 0.9 copy-start.2
  4.5 0.7 copy-start.4

commit v2 on v1

--- a/solution.py
+++ b/solution.py
@@ -14,7 +14,7 @@
 D = 1024
 CH = D // K
 N = 512
-DMON, MIX, DMIX, MON = 0, 1, 2, 3
+DMON, DMIX, MIX, MON = 0, 1, 2, 3
 NT = (((1,), (1,)), ((), ()))
 
 
@@ -35,12 +35,12 @@
 
 
 def kernel(
-    x_hbm, c_hbm, r_hbm, l_ref, gi_ref, go_ref,
-    o_hbm, dr_hbm, dl_ref, dgi_ref, dgo_ref,
-    xv, cv, hv, p1, dh, out, rr, rt, ww, wt,
-    tbuf, sbuf, rbuf, racc, lacc, gacc,
-    gxs, gxr, gys, gyr, fin, drv, lx, ly, ga, gb, gc,
-    in_sem, out_sem, ys, yr, zs, zr, rs_s, rs_r, sm_s, sm_r,
+    x_hbm, c_hbm, r_hbm, l_hbm, gi_hbm, go_hbm,
+    o_ref, dr_ref, dl_ref, dgi_ref, dgo_ref,
+    l_ref, gi_ref, go_ref, xv, cv, hv, p1, dh, rr, rt, ww, wt,
+    tbuf, sbuf, rbuf, racc, lacc,
+    gxs, gxr, gys, gyr, fin, lx, lxr, ly, lf, ga, gb, gc,
+    in_sem, ys, yr, zs, zr, rs_s, rs_r, sm_s, sm_r,
 ):
     dp = lax.axis_index("dp")
     seq = lax.axis_index("seq")
@@ -70,7 +70,17 @@
     def load_r(h):
         return pltpu.make_async_copy(r_hbm.at[:, h], rr.at[h], in_sem.at[2 * K + h])
 
-    for k in range(K):
+    def load_small():
+        pairs = ((l_hbm, l_ref), (gi_hbm, gi_ref), (go_hbm, go_ref))
+        return [
+            pltpu.make_async_copy(a, b, in_sem.at[2 * K + 2 + i]) for i, (a, b) in enumerate(pairs)
+        ]
+
+    load_x(0).start()
+    load_c(0).start()
+    for copy in load_small():
+        copy.start()
+    for k in range(1, K):
         load_x(k).start()
         load_c(k).start()
     for h in range(2):
@@ -104,14 +114,14 @@
     def y_arrived(s):
         pltpu.make_async_copy(sbuf.at[s, oth], sbuf.at[s, oth], yr.at[s]).wait()
 
-    def z_send(s):
-        pltpu.make_async_copy(sbuf.at[s, :, me], rbuf.at[s, :, me], zr.at[s]).start()
+    def z_send(s, h):
+        pltpu.make_async_copy(sbuf.at[s, h, me], rbuf.at[s, h, me], zr.at[s]).start()
 
         def step(i, _):
             q = lax.rem(me + i, 16)
             pltpu.make_async_remote_copy(
-                src_ref=sbuf.at[s, :, q],
-                dst_ref=rbuf.at[s, :, me],
+                src_ref=sbuf.at[s, h, q],
+                dst_ref=rbuf.at[s, h, me],
                 send_sem=zs.at[s],
                 recv_sem=zr.at[s],
                 device_id=zc_peer(q),
@@ -175,12 +185,18 @@
     def flat(s):
         return rbuf[s].reshape(N, CH)
 
+    def launch(s):
+        y_copy(s).start()
+        z_send(s, yh)
+
     def on_dmon(k):
         make_halves(DMIX * K + k, wt, flat(DMON * K + k))
+        launch(DMIX * K + k)
 
     def on_mix(k):
         m = flat(MIX * K + k)
         make_halves(MON * K + k, ww, m)
+        launch(MON * K + k)
         lacc[...] += dot_nt(m, flat(DMON * K + k))
 
     def fold(v):
@@ -196,10 +212,7 @@
             return acc + fold(dh[k, row, :] * xv[k, row, :].astype(F32))
 
         acc = lax.fori_loop(0, 16, step, jnp.zeros((8, CH), F32))
-        gacc[k, 0:1, :] = acc.sum(axis=0, keepdims=True)
-
-    def store_out(k):
-        return pltpu.make_async_copy(out.at[k], o_hbm.at[0, :, pl.ds(k * CH, CH)], out_sem.at[k])
+        ga[0, me, k] = acc.sum(axis=0, keepdims=True)
 
     def on_mon(k):
         gi, go = gates(k)
@@ -210,11 +223,11 @@
             mon = rbuf[MON * K + k, h, pl.ds(w * 2, 2)].reshape(32, CH).astype(F32)
             dpre = p1[k, row, :] * mon
             gg = (dpre * go).astype(BF16).astype(F32)
-            out[k, row, :] = (gg + dh[k, row, :] * gi).astype(BF16)
+            o_ref[0, row, k * CH : (k + 1) * CH] = (gg + dh[k, row, :] * gi).astype(BF16)
             return acc + fold(dpre * xv[k, row, :].astype(F32))
 
         acc = lax.fori_loop(0, 16, step, jnp.zeros((8, CH), F32))
-        gacc[k, 1:2, :] = acc.sum(axis=0, keepdims=True)
+        ga[1, me, k] = acc.sum(axis=0, keepdims=True)
 
     def spread(buf, i_sem, peer_of, mine, n):
         def step(i, _):
@@ -276,15 +289,30 @@
         mid = rest.astype(BF16)
         return hi, mid, (rest - mid.astype(F32)).astype(BF16)
 
-    def left_grad():
+    def left_1():
         r, c = iota((N, N), 0), iota((N, N), 1)
         kept = jnp.where(r % 16 == c % 16, lacc[...], 0.0)
         e = (iota((32, N), 0) == iota((32, N), 1) // 16).astype(F32).astype(BF16)
         hi, mid, low = split(kept)
-        lx[xx] = dot(e, hi) + dot(e, mid) + dot(e, low)
+        lx[...] = (dot(e, hi) + dot(e, mid) + dot(e, low)).reshape(4, 8, N)
+        scatter(lx, lxr, 2, x_peer, xx)
+
+    def left_2():
+        scatter_wait(lx, lxr, 2)
+        own = lx[xx]
+        for i in range(1, 4):
+            own = own + lxr[lax.rem(xx + i, 4)]
+        ly[yl] = own
+        spread(ly, 0, yl_peer, yl, 4)
+
+    def left_3():
+        spread_wait(ly, 0, 4)
+        lf[xx] = (ly[0] + ly[1] + ly[2] + ly[3]) * (1.0 / 128.0)
+        spread(lf, 1, x_peer, xx, 4)
 
     def left_out():
-        g = (ly[0] + ly[1] + ly[2] + ly[3]) * (1.0 / 128.0)
+        spread_wait(lf, 1, 4)
+        g = lf[...].reshape(32, N)
         r, c = iota((N, N), 0), iota((N, N), 1)
         perm = ((c % 16 == r // 32) & (natural(c // 16) == r % 32)).astype(F32).astype(BF16)
         cols = (natural(iota((32, 32), 0)) == iota((32, 32), 1)).astype(F32).astype(BF16)
@@ -318,133 +346,150 @@
         spread_wait(fin.at[xx], 2, 4)
         spread(fin, 3, x_peer, xx, 4)
 
-    right_store = pltpu.make_async_copy(drv, dr_hbm, out_sem.at[K])
-
     def right_5():
         spread_wait(fin, 3, 4)
 
         def step(j, _):
-            drv[j % 8, j // 8] = fin[j // 4, j % 4].astype(F32)
+            dr_ref[j % 8, j // 8] = fin[j // 4, j % 4].astype(F32)
             return 0
 
         lax.fori_loop(0, 16, step, 0)
-        right_store.start()
+
+    def gate_1(g):
+        spread(ga.at[g], 4 + g, zc_peer, me, 16)
+
+    def gate_2(g):
+        spread_wait(ga.at[g], 4 + g, 16)
+        gb[g, xx] = ga[g].sum(axis=0)
+        spread(gb.at[g], 6 + g, x_peer, xx, 4)
+
+    def gate_3(g):
+        spread_wait(gb.at[g], 6 + g, 4)
+        gc[g, ring] = gb[g].sum(axis=0)
+        spread(gc.at[g], 8 + g, y_peer, ring, 8)
+
+    def gate_4(g, out_ref):
+        spread_wait(gc.at[g], 8 + g, 8)
+        total = gc[g].sum(axis=0) * (1.0 / 512.0)
+        for k in range(K):
+            out_ref[:, k * CH : (k + 1) * CH] = total[k]
 
     lacc[...] = jnp.zeros_like(lacc)
     racc[...] = jnp.zeros_like(racc)
+    for copy in load_small():
+        copy.wait()
     for k in range(K):
         load_x(k).wait()
         load_c(k).wait()
         make_dmon(k, oth, False)
-        if k == 0:
-            pl.semaphore_wait(barrier, 25)
-        if k < 2:
-            y_copy(k).start()
         make_dmon(k, yh, True)
+    pl.semaphore_wait(barrier, 25)
+    y_copy(0).start()
+    z_send(0, yh)
+    z_send(1, yh)
+    y_copy(1).start()
+    z_send(2, yh)
+    z_send(3, yh)
     for h in range(2):
         load_r(h).wait()
-    make_mix(0)
     build_left()
+    for k in range(K):
+        make_mix(k)
 
     last = 4 * K
 
     def slot(t):
         y_arrived(t)
-
-        @pl.when(t + 2 < last)
-        def _():
-            y_copy(t + 2).start()
-
-        z_send(t)
+        z_send(t, oth)
+
+    def after(t, on, k):
+        z_arrived(t)
+        on(k)
 
     slot(0)
-
-    def phase_dmon(k, _):
-        make_mix(k)
-        slot(DMON * K + k)
-        z_arrived(DMON * K + k - 1)
-        on_dmon(k - 1)
+    y_copy(2).start()
+    z_send(8, yh)
+    slot(1)
+    y_copy(3).start()
+    z_send(9, yh)
+    after(0, on_dmon, 0)
+    slot(2)
+    z_send(10, yh)
+    after(1, on_dmon, 1)
+    slot(3)
+    z_send(11, yh)
+    after(2, on_dmon, 2)
+    slot(4)
+    after(3, on_dmon, 3)
+
+    def middle(k, _):
+        slot(DMIX * K + k)
+        y_copy(MIX * K + k - 1).start()
+        after(DMIX * K + k - 1, on_dmix, k - 1)
         return 0
 
-    lax.fori_loop(1, K, phase_dmon, 0)
-    slot(MIX * K)
-    z_arrived(MIX * K - 1)
-    on_dmon(K - 1)
-
-    def phase_mix(k, _):
-        slot(MIX * K + k)
-        z_arrived(MIX * K + k - 1)
-        on_mix(k - 1)
-        return 0
-
-    lax.fori_loop(1, K, phase_mix, 0)
-    slot(DMIX * K)
-    z_arrived(DMIX * K - 1)
-    on_mix(K - 1)
-    left_grad()
-    spread(lx, 0, x_peer, xx, 4)
-
-    def phase_dmix(k, _):
-        slot(DMIX * K + k)
-        z_arrived(DMIX * K + k - 1)
-        on_dmix(k - 1)
-        return 0
-
-    lax.fori_loop(1, K, phase_dmix, 0)
-    spread_wait(lx, 0, 4)
-    ly[yl] = lx[0] + lx[1] + lx[2] + lx[3]
-    spread(ly, 1, yl_peer, yl, 4)
-
-    slot(MON * K)
-    z_arrived(MON * K - 1)
-    on_dmix(K - 1)
+    lax.fori_loop(1, K, middle, 0)
+    slot(8)
+    y_copy(11).start()
+    after(7, on_dmix, 3)
     right_1()
-    for k in range(1, K):
-        slot(MON * K + k)
-        z_arrived(MON * K + k - 1)
-        on_mon(k - 1)
-        store_out(k - 1).start()
-        if k == 1:
-            right_2()
-            spread_wait(ly, 1, 4)
-            left_out()
-        if k == 2:
-            right_3()
-        if k == 3:
-            right_4()
-    z_arrived(last - 1)
-    on_mon(K - 1)
-    store_out(K - 1).start()
-    ga[me] = jnp.concatenate([gacc[k] for k in range(K)], axis=1)
-    spread(ga, 4, zc_peer, me, 16)
+    gate_1(0)
+    slot(9)
+    after(8, on_mix, 0)
+    slot(10)
+    after(9, on_mix, 1)
+    slot(11)
+    after(10, on_mix, 2)
+    right_2()
+    gate_2(0)
+    slot(12)
+    after(11, on_mix, 3)
+    left_1()
+    slot(13)
+    gate_3(0)
+    after(12, on_mon, 0)
+    slot(14)
+    after(13, on_mon, 1)
+    right_3()
+    left_2()
+    slot(15)
+    after(14, on_mon, 2)
+    right_4()
+    left_3()
+    gate_4(0, dgi_ref)
+    after(15, on_mon, 3)
+    gate_1(1)
+    gate_2(1)
     right_5()
-    spread_wait(ga, 4, 16)
-    gb[xx] = ga[...].sum(axis=0)
-    spread(gb, 5, x_peer, xx, 4)
-    spread_wait(gb, 5, 4)
-    gc[ring] = gb[...].sum(axis=0)
-    spread(gc, 6, y_peer, ring, 8)
-    spread_wait(gc, 6, 8)
-    total = gc[...].sum(axis=0) * (1.0 / 512.0)
-    dgi_ref[...] = total[0:1]
-    dgo_ref[...] = total[1:2]
+    gate_3(1)
+    left_out()
     lax.fori_loop(0, last, sends_done, 0)
-    for k in range(K):
-        store_out(k).wait()
-    right_store.wait()
+    gate_4(1, dgo_ref)
+
+
+def copy_kernel(*refs):
+    n = len(refs) // 2
+    sem = refs[-1]
+    copies = [pltpu.make_async_copy(refs[i], refs[n + i], sem.at[i]) for i in range(n)]
+    for copy in copies:
+        copy.start()
+    for copy in copies:
+        copy.wait()
 
 
 def on_device(inputs, cotangent, block_right, block_left, gate_in, gate_out):
-    hbm = pl.BlockSpec(memory_space=pl.ANY)
+    hbm = pl.BlockSpec(memory_space=pltpu.HBM)
     vmem = pl.BlockSpec(memory_space=pltpu.VMEM)
     sub = 4 * K
     scratch = [
+        pltpu.VMEM((16, 32, 32), BF16),
+        pltpu.VMEM((1, D), F32),
+        pltpu.VMEM((1, D), F32),
         pltpu.VMEM((K, N, CH), BF16),
         pltpu.VMEM((K, N, CH), BF16),
         pltpu.VMEM((K, N, CH), BF16),
         pltpu.VMEM((K, N, CH), F32),
         pltpu.VMEM((K, N, CH), F32),
-        pltpu.VMEM((K, N, CH), BF16),
         pltpu.VMEM((2, 8, 32, N), BF16),
         pltpu.VMEM((N, N), BF16),
         pltpu.VMEM((2, 256, N), BF16),
@@ -454,53 +499,66 @@
         pltpu.VMEM((sub, 2, 16, 16, CH), BF16),
         pltpu.VMEM((N, N), F32),
         pltpu.VMEM((N, N), F32),
-        pltpu.VMEM((K, 2, CH), F32),
         pltpu.VMEM((4, 128, N), BF16),
         pltpu.VMEM((4, 128, N), BF16),
         pltpu.VMEM((4, 32, N), BF16),
         pltpu.VMEM((4, 32, N), BF16),
         pltpu.VMEM((4, 4, 32, N), BF16),
-        pltpu.VMEM((8, 2, 32, N), F32),
-        pltpu.VMEM((4, 32, N), F32),
-        pltpu.VMEM((4, 32, N), F32),
-        pltpu.VMEM((16, 2, D), F32),
-        pltpu.VMEM((4, 2, D), F32),
-        pltpu.VMEM((8, 2, D), F32),
-        pltpu.SemaphoreType.DMA((2 * K + 2,)),
-        pltpu.SemaphoreType.DMA((K + 1,)),
+        pltpu.VMEM((4, 8, N), F32),
+        pltpu.VMEM((4, 8, N), F32),
+        pltpu.VMEM((4, 8, N), F32),
+        pltpu.VMEM((4, 8, N), F32),
+        pltpu.VMEM((2, 16, K, 1, CH), F32),
+        pltpu.VMEM((2, 4, K, 1, CH), F32),
+        pltpu.VMEM((2, 8, K, 1, CH), F32),
+        pltpu.SemaphoreType.DMA((2 * K + 5,)),
         pltpu.SemaphoreType.DMA((sub,)),
         pltpu.SemaphoreType.DMA((sub,)),
         pltpu.SemaphoreType.DMA((sub,)),
         pltpu.SemaphoreType.DMA((sub,)),
-        pltpu.SemaphoreType.DMA((2,)),
-        pltpu.SemaphoreType.DMA((2,)),
-        pltpu.SemaphoreType.DMA((7,)),
-        pltpu.SemaphoreType.DMA((7,)),
+        pltpu.SemaphoreType.DMA((3,)),
+        pltpu.SemaphoreType.DMA((3,)),
+        pltpu.SemaphoreType.DMA((10,)),
+        pltpu.SemaphoreType.DMA((10,)),
     ]
-    d_inputs, d_right, d_left, d_gin, d_gout = pl.pallas_call(
+    shapes = (
+        ((1, N, D), BF16),
+        ((8, 2, 32, N), F32),
+        ((16, 32, 32), F32),
+        ((1, D), F32),
+        ((1, D), F32),
+    )
+    results = pl.pallas_call(
         kernel,
-        out_shape=(
-            jax.ShapeDtypeStruct((1, N, D), BF16),
-            jax.ShapeDtypeStruct((8, 2, 32, N), F32),
-            jax.ShapeDtypeStruct((16, 32, 32), F32),
-            jax.ShapeDtypeStruct((1, D), F32),
-            jax.ShapeDtypeStruct((1, D), F32),
-        ),
-        in_specs=[hbm, hbm, hbm, vmem, vmem, vmem],
-        out_specs=(hbm, hbm, vmem, vmem, vmem),
+        out_shape=tuple(pltpu.VMEM(*shape) for shape in shapes),
+        in_specs=[hbm] * 6,
+        out_specs=(vmem,) * 5,
         scratch_shapes=scratch,
         compiler_params=pltpu.CompilerParams(
             collective_id=0, has_side_effects=True, vmem_limit_bytes=50 * 1024 * 1024
         ),
         name="monarch",
     )(
-        inputs,
-        cotangent,
-        block_right.reshape(8, 2, 32, N),
-        block_left,
-        gate_in.reshape(1, D),
-        gate_out.reshape(1, D),
+        *(
+            pltpu.with_memory_space_constraint(a, pltpu.HBM)
+            for a in (
+                inputs,
+                cotangent,
+                block_right.reshape(8, 2, 32, N),
+                block_left,
+                gate_in.reshape(1, D),
+                gate_out.reshape(1, D),
+            )
+        )
     )
+    d_inputs, d_right, d_left, d_gin, d_gout = pl.pallas_call(
+        copy_kernel,
+        out_shape=tuple(jax.ShapeDtypeStruct(*shape) for shape in shapes),
+        in_specs=[vmem] * 5,
+        out_specs=(hbm,) * 5,
+        scratch_shapes=[pltpu.SemaphoreType.DMA((5,))],
+        name="results",
+    )(*(pltpu.with_memory_space_constraint(r, pltpu.VMEM) for r in results))
     return (
         d_inputs,
         d_right.reshape(1, N, N),

time: 159 us -> 138 us (0.87)
  Pallas kernels: 149 us -> 137 us
  local copies, waits for them, and re-layouts: 8.37 us -> 0 us
    pallas_call x1 -> x2, Pallas kernels: 149 us -> 137 us  [the longest x1 135 us: on_device(): pl.pallas_call(kernel, out_shape=tuple((pltpu.VMEM(*shape) for shape in s...]
    unnamed x15 -> x0, local copies, waits for them, and re-layouts: 8.37 us -> none
where the time goes in v2:
time: 138 us
  Pallas kernels  137 us (99%)
    pallas_call x1, Pallas kernels, on_device(): pl.pallas_call(kernel, out_shape=tuple((pltpu.VMEM(*shape) for shape in s...  135 us

profile of v2, /device:TPU:1, one launch (start us, length us, event | category | flops | bytes accessed | tf_op | source)
XLA Modules:
  0.0 137.6 jit_solution(2256403409100035974)
XLA Ops:
  0.6 135.5 %monarch.1 = (bf16[1,512,1024]{2,1,0:T(8,128)(2,1)S(1)}, f32[8,2,32,512]{3,2,1,0:T(8,128)S(1)}, f32[16,32,32]{2,1,0:T(8,128)S(1)}, f32[1,1024]{1,0:T(1,128)S(1)}, f32[1,1024]{1,0:T(1,128)S(1)}) custom-call(bf16[1,512,1024]{2,1,0:T(8,128)(2,1)} %x_hbm.1, bf16[1,512,1024]{2,1,0:T(8,128)(2,1)} %c_hbm.1, bf16[8,2,32,512]{3,2,1,0:T(8,128)(2,1)} %bitcast.6, ...), custom_call_target="tpu_custom_call" | custom-call | tf_op jit(solution)/shard_map/monarch/pallas_call | solution.py:531
  136.1 1.4 %results.1 = (bf16[1,512,1024]{2,1,0:T(8,128)(2,1)}, f32[8,2,32,512]{3,2,1,0:T(8,128)}, f32[16,32,32]{2,1,0:T(8,128)}, f32[1,1024]{1,0:T(1,128)}, f32[1,1024]{1,0:T(1,128)}) custom-call(bf16[1,512,1024]{2,1,0:T(8,128)(2,1)S(1)} %get-tuple-element.15.refs_0_, f32[8,2,32,512]{3,2,1,0:T(8,128)S(1)} %get-tuple-element.16.refs_1_, ...), custom_call_target="tpu_custom_call" | custom-call | tf_op jit(solution)/shard_map/results/pallas_call | solution.py:554

commit v3 on v2

--- a/solution.py
+++ b/solution.py
@@ -10,7 +10,7 @@
 MESH = pl.DeviceIdType.MESH
 F32 = jnp.float32
 BF16 = jnp.bfloat16
-K = 4
+K = 8
 D = 1024
 CH = D // K
 N = 512
@@ -80,26 +80,26 @@
     load_c(0).start()
     for copy in load_small():
         copy.start()
+
+    barrier = pltpu.get_barrier_semaphore()
+
+    def greet(peer_of, mine, n):
+        def step(i, _):
+            pl.semaphore_signal(
+                barrier, inc=1, device_id=peer_of(lax.rem(mine + i, n)), device_id_type=MESH
+            )
+            return 0
+
+        lax.fori_loop(1, n, step, 0)
+
+    greet(zc_peer, me, 16)
+    greet(x_peer, xx, 4)
+    greet(y_peer, ring, 8)
     for k in range(1, K):
         load_x(k).start()
         load_c(k).start()
     for h in range(2):
         load_r(h).start()
-
-    barrier = pltpu.get_barrier_semaphore()
-
-    def greet(peer_of, mine, n):
-        def step(i, _):
-            pl.semaphore_signal(
-                barrier, inc=1, device_id=peer_of(lax.rem(mine + i, n)), device_id_type=MESH
-            )
-            return 0
-
-        lax.fori_loop(1, n, step, 0)
-
-    greet(zc_peer, me, 16)
-    greet(x_peer, xx, 4)
-    greet(y_peer, ring, 8)
 
     def y_copy(s):
         return pltpu.make_async_remote_copy(
@@ -139,9 +139,11 @@
         pltpu.make_async_copy(sbuf.at[s, :, pl.ds(0, 15)], sbuf.at[s, :, pl.ds(0, 15)], zs.at[s]).wait()
         return 0
 
+    def lanes_of(k):
+        return pl.ds(pl.multiple_of(k * CH, CH), CH)
+
     def gates(k):
-        lanes = pl.ds(pl.multiple_of(k * CH, CH), CH)
-        return gi_ref[:, lanes], go_ref[:, lanes]
+        return gi_ref[:, lanes_of(k)], go_ref[:, lanes_of(k)]
 
     def make_dmon(k, h, mine):
         _, go = gates(k)
@@ -223,7 +225,7 @@
             mon = rbuf[MON * K + k, h, pl.ds(w * 2, 2)].reshape(32, CH).astype(F32)
             dpre = p1[k, row, :] * mon
             gg = (dpre * go).astype(BF16).astype(F32)
-            o_ref[0, row, k * CH : (k + 1) * CH] = (gg + dh[k, row, :] * gi).astype(BF16)
+            o_ref[0, row, lanes_of(k)] = (gg + dh[k, row, :] * gi).astype(BF16)
             return acc + fold(dpre * xv[k, row, :].astype(F32))
 
         acc = lax.fori_loop(0, 16, step, jnp.zeros((8, CH), F32))
@@ -360,109 +362,121 @@
 
     def gate_2(g):
         spread_wait(ga.at[g], 4 + g, 16)
-        gb[g, xx] = ga[g].sum(axis=0)
-        spread(gb.at[g], 6 + g, x_peer, xx, 4)
+        gc[g, ring] = ga[g].sum(axis=0)
+        spread(gc.at[g], 6 + g, y_peer, ring, 8)
 
     def gate_3(g):
-        spread_wait(gb.at[g], 6 + g, 4)
-        gc[g, ring] = gb[g].sum(axis=0)
-        spread(gc.at[g], 8 + g, y_peer, ring, 8)
+        spread_wait(gc.at[g], 6 + g, 8)
+        gb[g, xx] = gc[g].sum(axis=0)
+        spread(gb.at[g], 8 + g, x_peer, xx, 4)
 
     def gate_4(g, out_ref):
-        spread_wait(gc.at[g], 8 + g, 8)
-        total = gc[g].sum(axis=0) * (1.0 / 512.0)
+        spread_wait(gb.at[g], 8 + g, 4)
+        total = gb[g].sum(axis=0) * (1.0 / 512.0)
         for k in range(K):
             out_ref[:, k * CH : (k + 1) * CH] = total[k]
 
-    lacc[...] = jnp.zeros_like(lacc)
-    racc[...] = jnp.zeros_like(racc)
     for copy in load_small():
         copy.wait()
-    for k in range(K):
+    load_x(0).wait()
+    load_c(0).wait()
+    make_dmon(0, oth, False)
+    pl.semaphore_wait(barrier, 25)
+    y_copy(0).start()
+    make_dmon(0, yh, True)
+    z_send(0, yh)
+    for k in range(1, K):
         load_x(k).wait()
         load_c(k).wait()
         make_dmon(k, oth, False)
+        y_copy(k).start()
         make_dmon(k, yh, True)
-    pl.semaphore_wait(barrier, 25)
-    y_copy(0).start()
-    z_send(0, yh)
-    z_send(1, yh)
-    y_copy(1).start()
-    z_send(2, yh)
-    z_send(3, yh)
+        z_send(k, yh)
+
+    handlers = {DMON: on_dmon, DMIX: on_dmix, MIX: on_mix, MON: on_mon}
+
+    def slot(array, k):
+        y_arrived(array * K + k)
+        z_send(array * K + k, oth)
+
+    def done(array, k):
+        z_arrived(array * K + k)
+        handlers[array](k)
+
+    def loop(first, end, body):
+        def step(k, _):
+            body(k)
+            return 0
+
+        lax.fori_loop(first, end, step, 0)
+
+    for k in range(2):
+        slot(DMON, k)
     for h in range(2):
         load_r(h).wait()
     build_left()
-    for k in range(K):
+    lacc[...] = jnp.zeros_like(lacc)
+    racc[...] = jnp.zeros_like(racc)
+    for k in range(2):
         make_mix(k)
 
-    last = 4 * K
-
-    def slot(t):
-        y_arrived(t)
-        z_send(t, oth)
-
-    def after(t, on, k):
-        z_arrived(t)
-        on(k)
-
-    slot(0)
-    y_copy(2).start()
-    z_send(8, yh)
-    slot(1)
-    y_copy(3).start()
-    z_send(9, yh)
-    after(0, on_dmon, 0)
-    slot(2)
-    z_send(10, yh)
-    after(1, on_dmon, 1)
-    slot(3)
-    z_send(11, yh)
-    after(2, on_dmon, 2)
-    slot(4)
-    after(3, on_dmon, 3)
-
-    def middle(k, _):
-        slot(DMIX * K + k)
-        y_copy(MIX * K + k - 1).start()
-        after(DMIX * K + k - 1, on_dmix, k - 1)
-        return 0
-
-    lax.fori_loop(1, K, middle, 0)
-    slot(8)
-    y_copy(11).start()
-    after(7, on_dmix, 3)
+    def dmon_slot(k):
+        slot(DMON, k)
+        make_mix(k)
+        done(DMON, k - 2)
+
+    def dmix_slot(k):
+        slot(DMIX, k)
+        z_send(MIX * K + k, yh)
+        y_copy(MIX * K + k - 2).start()
+        done(DMIX, k - 2)
+
+    def mix_slot(k):
+        slot(MIX, k)
+        done(MIX, k - 2)
+
+    loop(2, K, dmon_slot)
+    for k in range(2):
+        slot(DMIX, k)
+        z_send(MIX * K + k, yh)
+        done(DMON, K - 2 + k)
+    loop(2, K, dmix_slot)
+    for k in range(2):
+        slot(MIX, k)
+        y_copy(MIX * K + K - 2 + k).start()
+        done(DMIX, K - 2 + k)
     right_1()
     gate_1(0)
-    slot(9)
-    after(8, on_mix, 0)
-    slot(10)
-    after(9, on_mix, 1)
-    slot(11)
-    after(10, on_mix, 2)
+    loop(2, K - 2, mix_slot)
     right_2()
     gate_2(0)
-    slot(12)
-    after(11, on_mix, 3)
+    loop(K - 2, K, mix_slot)
+    for k in range(2):
+        slot(MON, k)
+        done(MIX, K - 2 + k)
     left_1()
-    slot(13)
+    for k in range(2, K - 2):
+        slot(MON, k)
+        done(MON, k - 2)
+        if k == 4:
+            left_2()
+    slot(MON, K - 2)
+    slot(MON, K - 1)
+    right_3()
     gate_3(0)
-    after(12, on_mon, 0)
-    slot(14)
-    after(13, on_mon, 1)
-    right_3()
-    left_2()
-    slot(15)
-    after(14, on_mon, 2)
+    done(MON, K - 4)
+    done(MON, K - 3)
     right_4()
     left_3()
+    done(MON, K - 2)
     gate_4(0, dgi_ref)
-    after(15, on_mon, 3)
+    done(MON, K - 1)
     gate_1(1)
     gate_2(1)
+    gate_3(1)
     right_5()
-    gate_3(1)
     left_out()
+    last = 4 * K
     lax.fori_loop(0, last, sends_done, 0)
     gate_4(1, dgo_ref)
 

time: 138 us -> 135 us (0.978)
  Pallas kernels: 137 us -> 134 us
    pallas_call x1, Pallas kernels: 135 us -> 133 us  [on_device(): pl.pallas_call(kernel, out_shape=tuple((pltpu.VMEM(*shape) for shape in s...]
where the time goes in v3:
time: 135 us
  Pallas kernels  134 us (99%)
    pallas_call x1, Pallas kernels, on_device(): pl.pallas_call(kernel, out_shape=tuple((pltpu.VMEM(*shape) for shape in s...  133 us

profile of v3, /device:TPU:1, one launch (start us, length us, event | category | flops | bytes accessed | tf_op | source)
XLA Modules:
  0.0 135.0 jit_solution(5087519989579331367)
XLA Ops:
  0.6 132.9 %monarch.1 = (bf16[1,512,1024]{2,1,0:T(8,128)(2,1)S(1)}, f32[8,2,32,512]{3,2,1,0:T(8,128)S(1)}, f32[16,32,32]{2,1,0:T(8,128)S(1)}, f32[1,1024]{1,0:T(1,128)S(1)}, f32[1,1024]{1,0:T(1,128)S(1)}) custom-call(bf16[1,512,1024]{2,1,0:T(8,128)(2,1)} %x_hbm.1, bf16[1,512,1024]{2,1,0:T(8,128)(2,1)} %c_hbm.1, bf16[8,2,32,512]{3,2,1,0:T(8,128)(2,1)} %bitcast.6, ...), custom_call_target="tpu_custom_call" | custom-call | tf_op jit(solution)/shard_map/monarch/pallas_call | solution.py:545
  133.5 1.4 %results.1 = (bf16[1,512,1024]{2,1,0:T(8,128)(2,1)}, f32[8,2,32,512]{3,2,1,0:T(8,128)}, f32[16,32,32]{2,1,0:T(8,128)}, f32[1,1024]{1,0:T(1,128)}, f32[1,1024]{1,0:T(1,128)}) custom-call(bf16[1,512,1024]{2,1,0:T(8,128)(2,1)S(1)} %get-tuple-element.15.refs_0_, f32[8,2,32,512]{3,2,1,0:T(8,128)S(1)} %get-tuple-element.16.refs_1_, ...), custom_call_target="tpu_custom_call" | custom-call | tf_op jit(solution)/shard_map/results/pallas_call | solution.py:568
